TPU v7x, 32 devices: a whole 2x2x4 slice. The times are simulated.
32 devices in a mesh: seq: 16 (over z, y, x), head: 2 (over core).
Axes of the slice: x: 2, y: 2, z: 4, core: 2. Of those that a mesh axis runs over, the one named last changes fastest.
Arguments:
- hidden: bfloat16 [2048, 2048], P('seq'), may hold values from -6 to 6
- queries: bfloat16 [2048, 3072], P('seq', 'head'), may hold values from -90 to 90
- req_len: int32 [2], replicated, may hold values from 1 to 1920, 2048 in all
- req_offset: int32 [2], replicated, may hold values from 0 to 4095
- expert_ids: int32 [2048, 6], P('seq'), may hold values from 0 to 15, all different within a row; in each aligned block of 128 rows (0 to 127, 128 to 255, ...) at most 64 rows name the same one
- decode_slot: int32 [128], replicated, may hold values from 0 to 127, as said below
- attn_gain: float32 [2048], replicated, may hold values from 0.25 to 1.75
- kv_down: bfloat16 [2048, 576], replicated, may hold values from -0.125 to 0.125
- kv_gain: float32 [512], replicated, may hold values from 0.25 to 1.75
- key_up: bfloat16 [16, 128, 512], P('head'), may hold values from -0.5 to 0.5
- value_up: bfloat16 [16, 512, 128], P('head'), may hold values from -0.25 to 0.25
- out_proj: bfloat16 [2048, 2048], P('head'), may hold values from -0.5 to 0.5
- ffn_gain: float32 [2048], replicated, may hold values from 0.25 to 1.75
- router: float32 [2048, 16], replicated, may hold values from -0.125 to 0.125
- expert_gate_up: bfloat16 [16, 2, 2048, 1408], P('seq', None, None, 'head'), may hold values from -0.125 to 0.125
- expert_down: bfloat16 [16, 1408, 2048], P('seq', 'head'), may hold values from -0.15625 to 0.15625
Outputs:
- output: bfloat16 [2048, 2048], P('seq', 'head')
- decode_latent: bfloat16 [128, 16, 512], P(('seq', 'head'))
- decode_rope: bfloat16 [128, 1024], P(('seq', 'head'))
Inputs may be any that keep to these rules, and one draw needn't show every extreme that they name: `req_len`: the lengths sum to 2048. `expert_ids`: the 128 rows of one index of seq name one expert at most 64 times in all. `decode_slot`: all entries differ; slot g belongs to device g // 4 in the order seq then head, and all 4 slots of some device are named.
All inputs are finite; a program needn't handle non-finite values.
Results may differ from a plain program's by a relative error of at most 0.02.
Values may be sent and summed in bfloat16 or wider, within the bound.
A program may use at most 128 MiB of HBM per device.

v0:
```python
import math
import jax
import jax.numpy as jnp
from jax import lax
from jax.sharding import PartitionSpec as P

D = 2048
NOPE = 128
ROPE = 64
V_HEAD = 128
KV_RANK = 512
TOP = 6
BLOCK = 16
DEC_SLOTS = 4
ROPE_BASE = 50000.0
ROUTE_SCALE = 2.446
EPSILON = 1e-06
MASKED = -1e30


def rms_rows(values, scale_gain):
    values = values.astype(jnp.float32)
    inverse = lax.rsqrt(jnp.mean(values * values, axis=-1, keepdims=True) + EPSILON)
    return values * inverse * scale_gain


def angles(position, rope_width):
    half_width = rope_width // 2
    freq_steps = jnp.arange(half_width).astype(jnp.float32) * (2.0 / rope_width)
    frequency = jnp.exp(-math.log(ROPE_BASE) * freq_steps)
    return position.astype(jnp.float32)[:, None] * frequency[None, :]


def rotate(values, rot_angle):
    half_width = values.shape[-1] // 2
    first_half = values[..., :half_width].astype(jnp.float32)
    second_half = values[..., half_width:].astype(jnp.float32)
    cosine = jnp.cos(rot_angle)
    sine_part = jnp.sin(rot_angle)
    return jnp.concatenate(
        [
            first_half * cosine - second_half * sine_part,
            first_half * sine_part + second_half * cosine,
        ],
        axis=-1,
    )


def request_of(req_len, token_index):
    req_ends = jnp.cumsum(req_len)
    return jnp.sum((token_index[:, None] >= req_ends[None, :]).astype(jnp.int32), axis=1)


def position_of(req_len, req_offset, token_index):
    request = request_of(req_len, token_index)
    req_ends = jnp.cumsum(req_len)
    starts = req_ends - req_len
    member = request[:, None] == jnp.arange(req_len.shape[0])[None, :]
    start_at = jnp.sum(jnp.where(member, starts[None, :], 0), axis=1)
    offset = jnp.sum(jnp.where(member, req_offset[None, :], 0), axis=1)
    return offset + token_index - start_at


def key_width(piece_rows):
    for option_width in (1024, 512, 256, 128):
        return option_width
    return piece_rows


def body(
    hidden,
    queries,
    req_len,
    req_offset,
    expert_ids,
    decode_slot,
    attn_gain,
    kv_down,
    kv_gain,
    key_up,
    value_up,
    out_proj,
    ffn_gain,
    router,
    expert_gate_up,
    expert_down,
):
    head_count = lax.axis_size("head")
    seq_place = lax.axis_index("seq")
    head_place = lax.axis_index("head")
    tok_rows = hidden.shape[0]
    heads_here = key_up.shape[0]
    my_index = seq_place * tok_rows + jnp.arange(tok_rows, dtype=jnp.int32)
    my_request = request_of(req_len, my_index)
    my_turn = angles(position_of(req_len, req_offset, my_index), ROPE)
    normed = rms_rows(hidden, attn_gain).astype(jnp.bfloat16)
    head_view = queries.reshape(tok_rows, heads_here, NOPE + ROPE)
    query_rope = rotate(head_view[:, :, NOPE:], my_turn[:, None, :]).astype(jnp.bfloat16)
    query_latent = jnp.einsum(
        "thn,hnc->thc", head_view[:, :, :NOPE], key_up, preferred_element_type=jnp.float32
    ).astype(jnp.bfloat16)
    query_rows = tok_rows * heads_here
    flat_latent = query_latent.reshape(query_rows, KV_RANK)
    flat_rope = query_rope.reshape(query_rows, ROPE)
    row_token = jnp.repeat(my_index, heads_here)
    row_request = jnp.repeat(my_request, heads_here)
    score_scale = 1.0 / math.sqrt(NOPE + ROPE)
    my_device = seq_place * head_count + head_place
    slot_ids = my_device * DEC_SLOTS + jnp.arange(DEC_SLOTS, dtype=jnp.int32)
    block_ids = jnp.arange(decode_slot.shape[0], dtype=jnp.int32)
    slot_match = decode_slot[None, :] == slot_ids[:, None]
    source_block = jnp.sum(jnp.where(slot_match, block_ids[None, :], 0), axis=1)
    slot_filled = jnp.any(slot_match, axis=1)
    kv_full = jnp.dot(normed, kv_down, preferred_element_type=jnp.float32)
    latent = rms_rows(kv_full[:, :KV_RANK], kv_gain).astype(jnp.bfloat16)
    key_rope = rotate(kv_full[:, KV_RANK:], my_turn).astype(jnp.bfloat16)
    run_peak = jnp.full((query_rows,), MASKED, jnp.float32)
    run_total = jnp.zeros((query_rows,), jnp.float32)
    run_acc = jnp.zeros((query_rows, KV_RANK), jnp.float32)
    piece_latent = lax.all_gather(latent, "seq", axis=0, tiled=True)
    piece_rope = lax.all_gather(key_rope, "seq", axis=0, tiled=True)
    piece_rows = piece_latent.shape[0]
    block_width = key_width(piece_rows)

    def key_block(block_no, loop_state):
        peak_now, total_now, acc_now = loop_state
        offset_rows = block_no * block_width
        block_latent = lax.dynamic_slice_in_dim(piece_latent, offset_rows, block_width, 0)
        block_rope = lax.dynamic_slice_in_dim(piece_rope, offset_rows, block_width, 0)
        key_index = offset_rows + jnp.arange(block_width, dtype=jnp.int32)
        key_request = request_of(req_len, key_index)
        contract = (((1,), (1,)), ((), ()))
        scores = lax.dot_general(
            flat_latent, block_latent, contract, preferred_element_type=jnp.float32
        )
        scores = (
            scores
            + lax.dot_general(flat_rope, block_rope, contract, preferred_element_type=jnp.float32)
        ) * score_scale
        allowed = (key_index[None, :] <= row_token[:, None]) & (
            key_request[None, :] == row_request[:, None]
        )
        scores = jnp.where(allowed, scores, MASKED)
        new_peak = jnp.maximum(peak_now, jnp.max(scores, axis=1))
        exp_terms = jnp.where(allowed, jnp.exp(scores - new_peak[:, None]), 0.0)
        fade_factor = jnp.exp(peak_now - new_peak)
        total_now = total_now * fade_factor + jnp.sum(exp_terms, axis=1)
        acc_now = acc_now * fade_factor[:, None] + jnp.dot(
            exp_terms.astype(jnp.bfloat16), block_latent, preferred_element_type=jnp.float32
        )
        return (new_peak, total_now, acc_now)

    run_peak, run_total, run_acc = lax.fori_loop(
        0, piece_rows // block_width, key_block, (run_peak, run_total, run_acc)
    )
    block_count = piece_rows // BLOCK
    pick_matrix = (
        source_block[:, None] == jnp.arange(block_count, dtype=jnp.int32)[None, :]
    ) & slot_filled[:, None]
    pick_matrix = pick_matrix.astype(jnp.bfloat16)
    slot_latent = jnp.dot(
        pick_matrix,
        piece_latent.reshape(block_count, BLOCK * KV_RANK),
        preferred_element_type=jnp.float32,
    )
    slot_rope = jnp.dot(
        pick_matrix,
        piece_rope.reshape(block_count, BLOCK * ROPE),
        preferred_element_type=jnp.float32,
    )
    folded = (run_peak, run_total, run_acc, slot_latent, slot_rope)
    run_total = folded[1]
    run_acc = folded[2]
    slot_latent = folded[3]
    slot_rope = folded[4]
    attended = (
        (run_acc / run_total[:, None]).astype(jnp.bfloat16).reshape(tok_rows, heads_here, KV_RANK)
    )
    head_out = jnp.einsum(
        "thc,hcv->thv", attended, value_up, preferred_element_type=jnp.float32
    ).astype(jnp.bfloat16)
    attn_part = jnp.dot(
        head_out.reshape(tok_rows, heads_here * V_HEAD),
        out_proj,
        preferred_element_type=jnp.float32,
    )
    mixed_rows = hidden.astype(jnp.float32) + lax.psum(
        attn_part.astype(jnp.bfloat16), "head"
    ).astype(jnp.float32)
    moe_in = rms_rows(mixed_rows, ffn_gain).astype(jnp.bfloat16)
    expert_count = router.shape[1]
    capacity = max(2, tok_rows * TOP * 4 // (3 * expert_count))
    gate_score = jax.nn.sigmoid(
        jnp.dot(moe_in.astype(jnp.float32), router, precision=lax.Precision.HIGHEST)
    )
    expert_axis = jnp.arange(expert_count, dtype=jnp.int32)
    id_match = expert_ids[:, :, None] == expert_axis[None, None, :]
    chosen = jnp.sum(jnp.where(id_match, gate_score[:, None, :], 0.0), axis=2)
    gate_weight = ROUTE_SCALE * chosen / jnp.sum(chosen, axis=1, keepdims=True)
    flat_ids = expert_ids.reshape(-1)
    one_hot = (flat_ids[:, None] == expert_axis[None, :]).astype(jnp.int32)
    earlier = jnp.cumsum(one_hot, axis=0) - one_hot
    slot_rank = jnp.sum(earlier * one_hot, axis=1)
    flat_slot = flat_ids * capacity + slot_rank
    owner_token = jnp.repeat(jnp.arange(tok_rows, dtype=jnp.int32), TOP)
    slot_token = jnp.zeros((expert_count * capacity,), jnp.int32).at[flat_slot].set(owner_token)
    slot_used = jnp.zeros((expert_count * capacity,), jnp.bool_).at[flat_slot].set(True)
    send_rows = jnp.where(
        slot_used[:, None], moe_in[slot_token], jnp.zeros((), jnp.bfloat16)
    ).reshape(expert_count, capacity, D)
    gate_up_local = expert_gate_up[0]
    down_local = expert_down[0]
    quarter_cols = D // head_count
    arrived = lax.all_to_all(send_rows, "seq", split_axis=0, concat_axis=0, tiled=True)
    sources, item_count, width_cols = arrived.shape
    flat_rows = arrived.reshape(sources * item_count, width_cols)
    gate_part = jnp.dot(flat_rows, gate_up_local[0], preferred_element_type=jnp.float32)
    up_part = jnp.dot(flat_rows, gate_up_local[1], preferred_element_type=jnp.float32)
    activated = (jax.nn.silu(gate_part) * up_part).astype(jnp.bfloat16)
    part_out = (
        jnp.dot(activated, down_local, preferred_element_type=jnp.float32)
        .astype(jnp.bfloat16)
        .reshape(sources, item_count, width_cols)
    )
    returned = lax.all_to_all(part_out, "seq", split_axis=0, concat_axis=0, tiled=True)
    back_cols = returned.shape[2]
    picked = returned.reshape(expert_count * capacity, back_cols)[flat_slot].reshape(
        tok_rows, TOP, back_cols
    )
    weighted = jnp.sum(picked.astype(jnp.float32) * gate_weight[:, :, None], axis=1)
    moe_out = lax.psum_scatter(
        weighted.astype(jnp.bfloat16), "head", scatter_dimension=1, tiled=True
    ).astype(jnp.float32)
    residual_part = lax.dynamic_slice_in_dim(mixed_rows, head_place * quarter_cols, quarter_cols, 1)
    output = (residual_part + moe_out).astype(jnp.bfloat16)
    decode_latent = slot_latent.astype(jnp.bfloat16).reshape(DEC_SLOTS, BLOCK, KV_RANK)
    decode_rope = slot_rope.astype(jnp.bfloat16)
    return (output, decode_latent, decode_rope)


def solution(mesh):
    placed = (
        P("seq", None),
        P("seq", "head"),
        P(),
        P(),
        P("seq", None),
        P(),
        P(),
        P(),
        P(),
        P("head", None, None),
        P("head", None, None),
        P("head", None),
        P(),
        P(),
        P("seq", None, None, "head"),
        P("seq", "head", None),
    )
    return jax.shard_map(
        body,
        mesh=mesh,
        in_specs=placed,
        out_specs=(P("seq", "head"), P(("seq", "head"), None, None), P(("seq", "head"), None)),
        check_vma=False,
    )
```

profile of v0, /device:TPU:14, one launch (start us, length us, event | category | flops | bytes accessed | tf_op | source)
XLA Modules:
  0.0 398.2 jit_solution(13828456274183690813)
XLA Ops:
  8.6 2.7 fusion.47
  19.5 32.4 %all_gather.7 = bf16[2048,64]{0,1:T(8,128)(2,1)} all-gather(bf16[128,64]{0,1:T(8,128)(2,1)S(1)} %pad_maximum_fusion.1), channel_id=1, replica_groups=mesh['seq'=16,'head'=2] {'seq'}, dimensions={0}, use_global_device_ids=true | all-gather | bytes 278528 | tf_op jit(solution)/shard_map/all_gather | solution.py:121
  63.5 12.5 %all-gather.2.cloned.1.call-done = bf16[2048,512]{0,1:T(8,128)(2,1)} async-done(((bf16[128,512]{0,1:T(8,128)(2,1)}), bf16[2048,512]{0,1:T(8,128)(2,1)}) %all-gather.2.cloned.1.call-update) | async-done | bytes 2097168 | tf_op jit(solution)/shard_map/all_gather | solution.py:120
  76.1 4.0 copy.49
  80.0 20.3 %while.20 = (s32[]{:T(128)}, f32[1024]{0:T(1024)S(1)}, f32[1024]{0:T(1024)S(1)}, f32[1024,512]{1,0:T(8,128)}, s32[1,2]{1,0:T(1,128)}, /*index=5*/bf16[2048,512]{...) while((s32[]{:T(128)}, f32[1024]{0:T(1024)S(1)}, ...), condition=%wide.region_11.12_spmd.clone, body=%wide.region_7.11_spmd.clone.sunk | while | flops 2303208448 | bytes 58217812 | solution.py:153
  100.3 2.0 fusion.44
  102.4 2.2 convolution_convert_fusion.4
  106.6 3.6 scatter_custom_fusion
  110.4 3.4 scatter_custom_fusion.1
  113.8 12.2 %all-reduce.2.cloned.1.call-done = bf16[128,2048]{1,0:T(8,128)(2,1)} async-done(((bf16[128,2048]{1,0:T(8,128)(2,1)}), bf16[128,2048]{1,0:T(8,128)(2,1)}) %all-reduce.2.cloned.1.call-update) | async-done | bytes 524304 | tf_op jit(solution)/shard_map/psum | solution.py:187
  126.1 2.3 convert_add_fusion
  129.8 6.0 %gather_fusion = bf16[1024,2048]{1,0:T(8,128)(2,1)} fusion(bf16[128,2048]{1,0:T(8,128)(2,1)S(1)} %multiply_convert_fusion.1, s32[1024]{0:T(1024)S(1)} %fusion.60), kind=kCustom, calls=%fused_computation | custom fusion | bytes 8392704 | tf_op jit(solution)/shard_map/gather | solution.py:209
  135.9 2.5 broadcast_select_fusion
  138.4 98.9 %all_to_all.10 = bf16[16,64,2048]{2,1,0:T(8,128)(2,1)S(1)} all-to-all(bf16[16,64,2048]{2,1,0:T(8,128)(2,1)S(1)} %broadcast_select_fusion), channel_id=1, replica_groups=mesh['seq'=16,'head'=2] {'seq'}, dimensions={0} | all-to-all | bytes 8388608 | tf_op jit(solution)/shard_map/all_to_all | solution.py:214
  237.3 2.0 copy-done.5
  239.3 6.6 %fusion.28 = f32[1024,704]{0,1:T(8,128)} fusion(bf16[1024,2048]{1,0:T(8,128)(2,1)S(1)} %bitcast.84, bf16[1,2,2048,704]{2,3,1,0:T(8,128)(2,1)} %param.32), kind=kOutput, calls=%fused_computation.40 | convolution fusion | flops 2952790016 | bytes 9961472 | tf_op jit(solution)/shard_map/dot_general | solution.py:218
  245.9 11.3 %convolution_convert_fusion.1 = bf16[1024,2048]{1,0:T(8,128)(2,1)} fusion(bf16[1,704,2048]{2,1,0:T(8,128)(2,1)S(1)} %copy-done, f32[1024,704]{0,1:T(8,128)} %fusion.28, bf16[1024,2048]{1,0:T(8,128)(2,1)} %bitcast.85, bf16[1,2,2048,704]{2,3,1,0:T(8,128)(2,1)} %param.32), kind=kOutput, calls=%fused_computation.38 | convolution fusion | flops 5912002560 | bytes 17039360 | tf_op jit(solution)/shard_map/dot_general | solution.py:221
  257.2 6.5 %all-to-all-start.1 = ((bf16[16,64,2048]{2,1,0:T(8,128)(2,1)}), bf16[16,64,2048]{2,1,0:T(8,128)(2,1)}, u32[]{:S(2)}, u32[]{:S(2)}) async-start(bf16[16,64,2048]{2,1,0:T(8,128)(2,1)} %bitcast.83), calls=%async_computation.1 | async-start | bytes 8388608 | tf_op jit(solution)/shard_map/all_to_all | solution.py:225
  264.7 91.1 %all-to-all-done.1 = bf16[16,64,2048]{2,1,0:T(8,128)(2,1)} async-done(((bf16[16,64,2048]{2,1,0:T(8,128)(2,1)}), bf16[16,64,2048]{2,1,0:T(8,128)(2,1)}, u32[]{:S(2)}, u32[]{:S(2)}) %all-to-all-start.1) | async-done | bytes 4194336 | tf_op jit(solution)/shard_map/all_to_all | solution.py:225
  355.8 9.8 %gather_fusion.1 = bf16[768,2048]{1,0:T(8,128)(2,1)} fusion(bf16[1024,2048]{1,0:T(8,128)(2,1)} %bitcast.18, s32[1024]{0:T(1024)S(1)} %pad_clamp_fusion), kind=kCustom, calls=%fused_computation.1 | custom fusion | bytes 6294528 | tf_op jit(solution)/shard_map/gather | solution.py:227
  365.7 6.6 %reshape.294 = f32[128,6,2048]{2,1,0:T(8,128)} reshape(bf16[768,2048]{1,0:T(8,128)(2,1)} %gather_fusion.1) | data formatting | bytes 9437184 | tf_op jit(solution)/shard_map/convert_element_type | solution.py:230
  372.2 7.5 %multiply_reduce_fusion = bf16[128,2048]{1,0:T(8,128)(2,1)} fusion(f32[128,6,2048]{2,1,0:T(8,128)} %reshape.294, f32[128,6]{1,0:T(8,128)S(1)} %copy.57), kind=kLoop, calls=%fused_computation.36 | loop fusion | flops 2883584 | bytes 6818816 | tf_op jit(solution)/shard_map/reduce_sum | solution.py:230
  382.9 4.2 %reshape.291 = bf16[128,8192]{1,0:T(8,128)(2,1)} reshape(bf16[2048,512]{1,0:T(8,128)(2,1)} %get-tuple-element.499) | data formatting | bytes 4194304 | tf_op jit(solution)/shard_map/reshape | solution.py:163
  387.1 2.0 convolution_convert_fusion
  (136 shorter events, 51.5 us)
Async XLA Ops:
  7.2 238.7 %copy-start = (bf16[1,704,2048]{2,1,0:T(8,128)(2,1)S(1)}, bf16[1,704,2048]{2,1,0:T(8,128)(2,1)}, u32[]{:S(2)}) copy-start(bf16[1,704,2048]{2,1,0:T(8,128)(2,1)} %param.33) | copy-start | bytes 8650756
  7.2 5.9 %copy-start.12 = (s32[128,6]{0,1:T(8,128)S(1)}, s32[128,6]{0,1:T(8,128)}, u32[]{:S(2)}) copy-start(s32[128,6]{0,1:T(8,128)} %param.22) | copy-start | bytes 9220
  7.2 6.8 %copy-start.17 = (s32[2]{0:T(128)S(1)}, s32[2]{0:T(128)}, u32[]{:S(2)}) copy-start(s32[2]{0:T(128)} %param.20) | copy-start | bytes 28
  7.2 11.4 %copy-start.16 = (s32[2]{0:T(128)S(1)}, s32[2]{0:T(128)}, u32[]{:S(2)}) copy-start(s32[2]{0:T(128)} %param.21) | copy-start | bytes 28
  7.2 68.8 %all-gather.2.cloned.1.call-start = ((), (), s32[]{:S(2)}) async-start(), calls=%async_computation.3 | async-start | bytes 2228224 | tf_op jit(solution)/shard_map/all_gather | solution.py:120
  13.0 113.1 %all-reduce.2.cloned.1.call-start = ((), (), s32[]{:S(2)}) async-start(), calls=%async_computation.4 | async-start | bytes 1048576 | tf_op jit(solution)/shard_map/psum | solution.py:187
  59.2 3.4 copy-start.8
  59.3 3.4 copy-start.9
  81.7 1.8 copy-start.3
  81.7 1.9 copy-start.10
  85.3 1.6 copy-start.6
  91.8 1.8 copy-start.3
  91.8 1.9 copy-start.10
  100.3 5.8 %copy-start.1 = (bf16[2048,64]{1,0:T(8,128)(2,1)}, bf16[2048,64]{1,0:T(8,128)(2,1)S(1)}, u32[]{:S(2)}) copy-start(bf16[2048,64]{1,0:T(8,128)(2,1)S(1)} %get-tuple-element.498) | copy-start | bytes 786436
  100.3 4.3 %copy-start.4 = (bf16[1024,2048]{1,0:T(8,128)(2,1)S(1)}, bf16[1024,2048]{1,0:T(8,128)(2,1)}, u32[]{:S(2)}) copy-start(bf16[1024,2048]{1,0:T(8,128)(2,1)} %param.29) | copy-start | bytes 12582916
  102.4 4.1 %copy-start.13 = (s32[768]{0:T(1024)S(1)}, s32[768]{0:T(1024)}, u32[]{:S(2)}) copy-start(s32[768]{0:T(1024)} %eq.123) | copy-start | bytes 9220
  102.4 4.2 %copy-start.14 = (s32[768,1]{0,1:T(1,128)S(1)}, s32[768,1]{0,1:T(1,128)}, u32[]{:S(2)}) copy-start(s32[768,1]{0,1:T(1,128)} %mul.268) | copy-start | bytes 9220
  104.6 23.8 %copy-start.15 = (f32[2048]{0:T(1024)S(1)}, f32[2048]{0:T(1024)}, u32[]{:S(2)}) copy-start(f32[2048]{0:T(1024)} %param.30) | copy-start | bytes 24580
  237.3 2.0 copy-start.5
  257.2 6.8 %copy-start.11 = (f32[2048,16]{0,1:T(8,128)S(1)}, f32[2048,16]{0,1:T(8,128)}, u32[]{:S(2)}) copy-start(f32[2048,16]{0,1:T(8,128)} %param.31) | copy-start | bytes 393220
  257.2 98.7 %all-to-all-start.1 = ((bf16[16,64,2048]{2,1,0:T(8,128)(2,1)}), bf16[16,64,2048]{2,1,0:T(8,128)(2,1)}, u32[]{:S(2)}, u32[]{:S(2)}) async-start(bf16[16,64,2048]{2,1,0:T(8,128)(2,1)} %bitcast.83), calls=%async_computation.1 | async-start | bytes 8388608 | tf_op jit(solution)/shard_map/all_to_all | solution.py:225
  263.7 126.1 %reduce-scatter.2.cloned.1.call-start = ((), (), s32[]{:S(2)}) async-start(), calls=%async_computation.5 | async-start | bytes 786432 | tf_op jit(solution)/shard_map/reduce_scatter | solution.py:231
  372.2 7.5 %copy-start.2 = (bf16[2048,64]{1,0:T(8,128)(2,1)S(1)}, bf16[2048,64]{1,0:T(8,128)(2,1)}, u32[]{:S(2)}) copy-start(bf16[2048,64]{1,0:T(8,128)(2,1)} %copy-done.1) | copy-start | bytes 786436
  372.2 8.6 %copy-start.18 = (s32[128]{0:T(128)S(1)}, s32[128]{0:T(128)}, u32[]{:S(2)}) copy-start(s32[128]{0:T(128)} %param.23) | copy-start | bytes 1540
  (3 other events, 4.3 us)
Sparse Core Ops, SparseCore 0:
  13.1 62.9 all-gather.1
  106.3 19.6 all-reduce.1
  379.8 7.2 reduce-scatter.1
where the time goes:
time: 399 us; the launch traced here: 398 us
  blocking collectives  131 us (33%)
  waiting for transfers between devices  116 us (29%)
  local copies, waits for them, and re-layouts  56 us (14%)
  matrix products  41.4 us (10%)
  other arithmetic  32.5 us (8%)
  between operations  14 us (4%)
  starting transfers between devices  6.86 us (2%)
    all_to_all x1, blocking collectives, body(): lax.all_to_all(send_rows, 'seq', split_axis=0, concat_axis=0, tiled=True)  98.9 us
    all_to_all x1, waiting for transfers between devices, body(): lax.all_to_all(part_out, 'seq', split_axis=0, concat_axis=0, tiled=True)  91.1 us
    all_gather x1, blocking collectives, body(): piece_rope = lax.all_gather(key_rope, 'seq', axis=0, tiled=True)  32.4 us
    all_gather x1, waiting for transfers between devices, body(): piece_latent = lax.all_gather(latent, 'seq', axis=0, tiled=True)  12.5 us
    psum x1, waiting for transfers between devices, body(): lax.psum(attn_part.astype(jnp.bfloat16), 'head').astype(jnp.float32)  12.2 us
    dot_general x1, matrix products, body(): jnp.dot(activated, down_local, preferred_element_type=jnp.float32)  11.3 us
    unnamed x35, local copies, waits for them, and re-layouts  9.92 us
    gather x1, local copies, waits for them, and re-layouts, body(): returned.reshape(expert_count * capacity, back_cols)[flat_slot]  9.82 us
  transfers between devices with their start and end apart: 4, of which 3 were waited for; matrix products, arithmetic and copies ran while one was open for 9% of the time, Pallas kernels for 0%

commit v1 on v0

--- a/solution.py
+++ b/solution.py
@@ -16,6 +16,17 @@
 ROUTE_SCALE = 2.446
 EPSILON = 1e-06
 MASKED = -1e30
+
+
+def pass_along(value, axis, d):
+    size = lax.axis_size(axis)
+    route = [(i, (i + 1) % size) for i in range(size)]
+    pieces = [value]
+    for stride in range(1, size):
+        pieces = [lax.ppermute(pieces[0], axis, route), *pieces]
+    out = jnp.concatenate(pieces, axis=d)
+    places = (lax.axis_index(axis) + 1) * pieces[-1].shape[d]
+    return jnp.roll(out, places, axis=d)
 
 
 def rms_rows(values, scale_gain):
@@ -118,7 +129,7 @@
     run_total = jnp.zeros((query_rows,), jnp.float32)
     run_acc = jnp.zeros((query_rows, KV_RANK), jnp.float32)
     piece_latent = lax.all_gather(latent, "seq", axis=0, tiled=True)
-    piece_rope = lax.all_gather(key_rope, "seq", axis=0, tiled=True)
+    piece_rope = pass_along(key_rope, "seq", 0)
     piece_rows = piece_latent.shape[0]
     block_width = key_width(piece_rows)
 

time: 399 us -> 487 us (1.22)
  starting transfers between devices: 6.86 us -> 62.5 us
  blocking collectives: 131 us -> 98.9 us
  local copies, waits for them, and re-layouts: 56 us -> 84 us
  waiting for transfers between devices: 116 us -> 144 us
  other arithmetic: 32.5 us -> 37.5 us
    ppermute x0 -> x15, starting transfers between devices: none -> 55.6 us  [pass_along(): pieces = [lax.ppermute(pieces[0], axis, route), *pieces]]
    all_gather x1 -> x0, blocking collectives: 32.4 us -> none  [body(): piece_rope = lax.all_gather(key_rope, 'seq', axis=0, tiled=True)]
    unnamed x35 -> x85, local copies, waits for them, and re-layouts: 9.92 us -> 36.4 us
    ppermute x0 -> x15, waiting for transfers between devices: none -> 16.3 us  [pass_along(): pieces = [lax.ppermute(pieces[0], axis, route), *pieces]]
    psum x1, waiting for transfers between devices: 12.2 us -> 21.7 us  [body(): lax.psum(attn_part.astype(jnp.bfloat16), 'head').astype(jnp.float32)]
  transfers between devices with their start and end apart: 4 -> 19, of which waited for: 3 -> 15; matrix products, arithmetic and copies ran while one was open for 9% -> 13% of each run, Pallas kernels for 0% -> 0%
where the time goes in v1:
time: 487 us; the launch traced here: 484 us
  waiting for transfers between devices  144 us (30%)
  blocking collectives  98.9 us (20%)
  local copies, waits for them, and re-layouts  84 us (17%)
  starting transfers between devices  62.5 us (13%)
  matrix products  42.3 us (9%)
  other arithmetic  37.5 us (8%)
  between operations  14.1 us (3%)
    all_to_all x1, blocking collectives, body(): lax.all_to_all(send_rows, 'seq', split_axis=0, concat_axis=0, tiled=True)  98.9 us
    all_to_all x1, waiting for transfers between devices, body(): lax.all_to_all(part_out, 'seq', split_axis=0, concat_axis=0, tiled=True)  91.1 us
    ppermute x15, starting transfers between devices, pass_along(): pieces = [lax.ppermute(pieces[0], axis, route), *pieces]  55.6 us
    unnamed x85, local copies, waits for them, and re-layouts  36.4 us
    psum x1, waiting for transfers between devices, body(): lax.psum(attn_part.astype(jnp.bfloat16), 'head').astype(jnp.float32)  21.7 us
    ppermute x15, waiting for transfers between devices, pass_along(): pieces = [lax.ppermute(pieces[0], axis, route), *pieces]  16.3 us
    all_gather x1, waiting for transfers between devices, body(): piece_latent = lax.all_gather(latent, 'seq', axis=0, tiled=True)  15 us
    dot_general x1, matrix products, body(): jnp.dot(activated, down_local, preferred_element_type=jnp.float32)  11.3 us
  transfers between devices with their start and end apart: 19, of which 15 were waited for; matrix products, arithmetic and copies ran while one was open for 13% of the time, Pallas kernels for 0%

profile of v1, /device:TPU:14, one launch (start us, length us, event | category | flops | bytes accessed | tf_op | source)
XLA Modules:
  0.0 483.7 jit_solution(4462716957646552240)
XLA Ops:
  25.6 4.1 collective-permute-start.2
  31.8 4.1 collective-permute-start.3
  37.9 4.1 collective-permute-start.4
  44.0 4.1 collective-permute-start.5
  50.2 4.1 collective-permute-start.6
  56.3 4.1 collective-permute-start.7
  62.5 4.1 collective-permute-start.8
  68.0 4.1 collective-permute-start.9
  84.6 4.1 collective-permute-start.12
  90.2 4.2 collective-permute-start.13
  96.1 4.2 collective-permute-start.14
  135.9 15.0 %all-gather.2.cloned.1.call-done = bf16[2048,512]{0,1:T(8,128)(2,1)} async-done(((bf16[128,512]{0,1:T(8,128)(2,1)}), bf16[2048,512]{0,1:T(8,128)(2,1)}) %all-gather.2.cloned.1.call-update) | async-done | bytes 2097168 | tf_op jit(solution)/shard_map/all_gather | solution.py:131
  154.8 21.4 %while.20 = (s32[]{:T(128)}, f32[1024]{0:T(1024)S(1)}, f32[1024]{0:T(1024)S(1)}, f32[1024,512]{1,0:T(8,128)}, s32[1,2]{1,0:T(1,128)}, /*index=5*/bf16[2048,512]{...) while((s32[]{:T(128)}, f32[1024]{0:T(1024)S(1)}, ...), condition=%wide.region_11.12_spmd.clone, body=%wide.region_7.11_spmd.clone.sunk | while | flops 2303208448 | bytes 58217812 | solution.py:164
  189.8 21.7 %all-reduce.2.cloned.1.call-done = bf16[128,2048]{1,0:T(8,128)(2,1)} async-done(((bf16[128,2048]{1,0:T(8,128)(2,1)}), bf16[128,2048]{1,0:T(8,128)(2,1)}) %all-reduce.2.cloned.1.call-update) | async-done | bytes 524304 | tf_op jit(solution)/shard_map/psum | solution.py:198
  215.3 6.0 %gather_fusion = bf16[1024,2048]{1,0:T(8,128)(2,1)} fusion(bf16[128,2048]{1,0:T(8,128)(2,1)S(1)} %multiply_convert_fusion.1, s32[1024]{0:T(1024)S(1)} %fusion.60), kind=kCustom, calls=%fused_computation | custom fusion | bytes 8392704 | tf_op jit(solution)/shard_map/gather | solution.py:220
  223.8 98.9 %all_to_all.10 = bf16[16,64,2048]{2,1,0:T(8,128)(2,1)S(1)} all-to-all(bf16[16,64,2048]{2,1,0:T(8,128)(2,1)S(1)} %broadcast_select_fusion), channel_id=1, replica_groups=mesh['seq'=16,'head'=2] {'seq'}, dimensions={0} | all-to-all | bytes 8388608 | tf_op jit(solution)/shard_map/all_to_all | solution.py:225
  324.7 6.6 %fusion.28 = f32[1024,704]{0,1:T(8,128)} fusion(bf16[1024,2048]{1,0:T(8,128)(2,1)S(1)} %bitcast.84, bf16[1,2,2048,704]{2,3,1,0:T(8,128)(2,1)} %param.32), kind=kOutput, calls=%fused_computation.40 | convolution fusion | flops 2952790016 | bytes 9961472 | tf_op jit(solution)/shard_map/dot_general | solution.py:229
  331.3 11.3 %convolution_convert_fusion.1 = bf16[1024,2048]{1,0:T(8,128)(2,1)} fusion(bf16[1,704,2048]{2,1,0:T(8,128)(2,1)S(1)} %copy-done, f32[1024,704]{0,1:T(8,128)} %fusion.28, bf16[1024,2048]{1,0:T(8,128)(2,1)} %bitcast.85, bf16[1,2,2048,704]{2,3,1,0:T(8,128)(2,1)} %param.32), kind=kOutput, calls=%fused_computation.38 | convolution fusion | flops 5912002560 | bytes 17039360 | tf_op jit(solution)/shard_map/dot_general | solution.py:232
  342.6 6.5 %all-to-all-start.1 = ((bf16[16,64,2048]{2,1,0:T(8,128)(2,1)}), bf16[16,64,2048]{2,1,0:T(8,128)(2,1)}, u32[]{:S(2)}, u32[]{:S(2)}) async-start(bf16[16,64,2048]{2,1,0:T(8,128)(2,1)} %bitcast.83), calls=%async_computation.1 | async-start | bytes 8388608 | tf_op jit(solution)/shard_map/all_to_all | solution.py:236
  350.1 91.1 %all-to-all-done.1 = bf16[16,64,2048]{2,1,0:T(8,128)(2,1)} async-done(((bf16[16,64,2048]{2,1,0:T(8,128)(2,1)}), bf16[16,64,2048]{2,1,0:T(8,128)(2,1)}, u32[]{:S(2)}, u32[]{:S(2)}) %all-to-all-start.1) | async-done | bytes 4194336 | tf_op jit(solution)/shard_map/all_to_all | solution.py:236
  441.2 9.8 %gather_fusion.1 = bf16[768,2048]{1,0:T(8,128)(2,1)} fusion(bf16[1024,2048]{1,0:T(8,128)(2,1)} %bitcast.18, s32[1024]{0:T(1024)S(1)} %pad_clamp_fusion), kind=kCustom, calls=%fused_computation.1 | custom fusion | bytes 6294528 | tf_op jit(solution)/shard_map/gather | solution.py:238
  451.1 6.6 %reshape.294 = f32[128,6,2048]{2,1,0:T(8,128)} reshape(bf16[768,2048]{1,0:T(8,128)(2,1)} %gather_fusion.1) | data formatting | bytes 9437184 | tf_op jit(solution)/shard_map/convert_element_type | solution.py:241
  457.6 7.5 %multiply_reduce_fusion = bf16[128,2048]{1,0:T(8,128)(2,1)} fusion(f32[128,6,2048]{2,1,0:T(8,128)} %reshape.294, f32[128,6]{1,0:T(8,128)S(1)} %copy.57), kind=kLoop, calls=%fused_computation.36 | loop fusion | flops 2883584 | bytes 6818816 | tf_op jit(solution)/shard_map/reduce_sum | solution.py:241
  468.3 4.2 reshape.291
  (218 shorter events, 138.8 us)
Async XLA Ops:
  7.2 324.1 %copy-start = (bf16[1,704,2048]{2,1,0:T(8,128)(2,1)S(1)}, bf16[1,704,2048]{2,1,0:T(8,128)(2,1)}, u32[]{:S(2)}) copy-start(bf16[1,704,2048]{2,1,0:T(8,128)(2,1)} %param.33) | copy-start | bytes 8650756
  7.2 76.0 %copy-start.23 = (s32[128,6]{0,1:T(8,128)S(1)}, s32[128,6]{0,1:T(8,128)}, u32[]{:S(2)}) copy-start(s32[128,6]{0,1:T(8,128)} %param.22) | copy-start | bytes 9220
  7.2 143.7 %all-gather.2.cloned.1.call-start = ((), (), s32[]{:S(2)}) async-start(), calls=%async_computation.3 | async-start | bytes 2228224 | tf_op jit(solution)/shard_map/all_gather | solution.py:131
  16.0 3.7 collective-permute-start
  20.3 4.7 collective-permute-start.1
  25.6 5.5 %collective-permute-start.2 = (bf16[128,64]{0,1:T(8,128)(2,1)S(1)}, bf16[128,64]{0,1:T(8,128)(2,1)S(1)}, u32[]{:S(2)}, u32[]{:S(2)}) collective-permute-start(bf16[128,64]{0,1:T(8,128)(2,1)S(1)} %collective-permute-done.1), channel_id=1, source_target_pairs={{0,2},{2,4},{4,6},{6,8},{8,10},{10,12},{12,14},{14,16},{16,18},{18... | collective-permute-start | bytes 49160 | tf_op jit(solution)/shard_map/ppermute | solution.py:26
  31.8 5.5 %collective-permute-start.3 = (bf16[128,64]{0,1:T(8,128)(2,1)S(1)}, bf16[128,64]{0,1:T(8,128)(2,1)S(1)}, u32[]{:S(2)}, u32[]{:S(2)}) collective-permute-start(bf16[128,64]{0,1:T(8,128)(2,1)S(1)} %collective-permute-done.2), channel_id=1, source_target_pairs={{0,2},{2,4},{4,6},{6,8},{8,10},{10,12},{12,14},{14,16},{16,18},{18... | collective-permute-start | bytes 49160 | tf_op jit(solution)/shard_map/ppermute | solution.py:26
  37.9 5.5 %collective-permute-start.4 = (bf16[128,64]{0,1:T(8,128)(2,1)S(1)}, bf16[128,64]{0,1:T(8,128)(2,1)S(1)}, u32[]{:S(2)}, u32[]{:S(2)}) collective-permute-start(bf16[128,64]{0,1:T(8,128)(2,1)S(1)} %collective-permute-done.3), channel_id=1, source_target_pairs={{0,2},{2,4},{4,6},{6,8},{8,10},{10,12},{12,14},{14,16},{16,18},{18... | collective-permute-start | bytes 49160 | tf_op jit(solution)/shard_map/ppermute | solution.py:26
  44.0 5.5 %collective-permute-start.5 = (bf16[128,64]{0,1:T(8,128)(2,1)S(1)}, bf16[128,64]{0,1:T(8,128)(2,1)S(1)}, u32[]{:S(2)}, u32[]{:S(2)}) collective-permute-start(bf16[128,64]{0,1:T(8,128)(2,1)S(1)} %collective-permute-done.4), channel_id=1, source_target_pairs={{0,2},{2,4},{4,6},{6,8},{8,10},{10,12},{12,14},{14,16},{16,18},{18... | collective-permute-start | bytes 49160 | tf_op jit(solution)/shard_map/ppermute | solution.py:26
  50.2 5.5 %collective-permute-start.6 = (bf16[128,64]{0,1:T(8,128)(2,1)S(1)}, bf16[128,64]{0,1:T(8,128)(2,1)S(1)}, u32[]{:S(2)}, u32[]{:S(2)}) collective-permute-start(bf16[128,64]{0,1:T(8,128)(2,1)S(1)} %collective-permute-done.5), channel_id=1, source_target_pairs={{0,2},{2,4},{4,6},{6,8},{8,10},{10,12},{12,14},{14,16},{16,18},{18... | collective-permute-start | bytes 49160 | tf_op jit(solution)/shard_map/ppermute | solution.py:26
  56.3 5.5 %collective-permute-start.7 = (bf16[128,64]{0,1:T(8,128)(2,1)S(1)}, bf16[128,64]{0,1:T(8,128)(2,1)S(1)}, u32[]{:S(2)}, u32[]{:S(2)}) collective-permute-start(bf16[128,64]{0,1:T(8,128)(2,1)S(1)} %collective-permute-done.6), channel_id=1, source_target_pairs={{0,2},{2,4},{4,6},{6,8},{8,10},{10,12},{12,14},{14,16},{16,18},{18... | collective-permute-start | bytes 49160 | tf_op jit(solution)/shard_map/ppermute | solution.py:26
  62.5 5.5 %collective-permute-start.8 = (bf16[128,64]{0,1:T(8,128)(2,1)S(1)}, bf16[128,64]{0,1:T(8,128)(2,1)S(1)}, u32[]{:S(2)}, u32[]{:S(2)}) collective-permute-start(bf16[128,64]{0,1:T(8,128)(2,1)S(1)} %collective-permute-done.7), channel_id=1, source_target_pairs={{0,2},{2,4},{4,6},{6,8},{8,10},{10,12},{12,14},{14,16},{16,18},{18... | collective-permute-start | bytes 49160 | tf_op jit(solution)/shard_map/ppermute | solution.py:26
  68.0 15.2 %copy-start.19 = (bf16[128,64]{0,1:T(8,128)(2,1)}, bf16[128,64]{0,1:T(8,128)(2,1)S(1)}, u32[]{:S(2)}) copy-start(bf16[128,64]{0,1:T(8,128)(2,1)S(1)} %collective-permute-done.8) | copy-start | bytes 49156
  68.0 6.9 %collective-permute-start.9 = (bf16[128,64]{0,1:T(8,128)(2,1)S(1)}, bf16[128,64]{0,1:T(8,128)(2,1)S(1)}, u32[]{:S(2)}, u32[]{:S(2)}) collective-permute-start(bf16[128,64]{0,1:T(8,128)(2,1)S(1)} %collective-permute-done.8), channel_id=1, source_target_pairs={{0,2},{2,4},{4,6},{6,8},{8,10},{10,12},{12,14},{14,16},{16,18},{18... | collective-permute-start | bytes 49160 | tf_op jit(solution)/shard_map/ppermute | solution.py:26
  73.6 137.9 %all-reduce.2.cloned.1.call-start = ((), (), s32[]{:S(2)}) async-start(), calls=%async_computation.4 | async-start | bytes 1048576 | tf_op jit(solution)/shard_map/psum | solution.py:198
  74.9 5.5 %collective-permute-start.10 = (bf16[128,64]{0,1:T(8,128)(2,1)S(1)}, bf16[128,64]{0,1:T(8,128)(2,1)S(1)}, u32[]{:S(2)}, u32[]{:S(2)}) collective-permute-start(bf16[128,64]{0,1:T(8,128)(2,1)S(1)} %collective-permute-done.9), channel_id=1, source_target_pairs={{0,2},{2,4},{4,6},{6,8},{8,10},{10,12},{12,14},{14,16},{16,18},{18... | collective-permute-start | bytes 49160 | tf_op jit(solution)/shard_map/ppermute | solution.py:26
  80.4 14.8 %copy-start.21 = (bf16[128,64]{0,1:T(8,128)(2,1)}, bf16[128,64]{0,1:T(8,128)(2,1)S(1)}, u32[]{:S(2)}) copy-start(bf16[128,64]{0,1:T(8,128)(2,1)S(1)} %collective-permute-done.10) | copy-start | bytes 49156
  80.4 4.3 collective-permute-start.11
  84.6 5.6 %collective-permute-start.12 = (bf16[128,64]{0,1:T(8,128)(2,1)S(1)}, bf16[128,64]{0,1:T(8,128)(2,1)}, u32[]{:S(2)}, u32[]{:S(2)}) collective-permute-start(bf16[128,64]{0,1:T(8,128)(2,1)S(1)} %collective-permute-done.11), channel_id=1, source_target_pairs={{0,2},{2,4},{4,6},{6,8},{8,10},{10,12},{12,14},{14,16},{16,18},{18... | collective-permute-start | bytes 49160 | tf_op jit(solution)/shard_map/ppermute | solution.py:26
  90.2 5.9 %collective-permute-start.13 = (bf16[128,64]{0,1:T(8,128)(2,1)}, bf16[128,64]{0,1:T(8,128)(2,1)}, u32[]{:S(2)}, u32[]{:S(2)}) collective-permute-start(bf16[128,64]{0,1:T(8,128)(2,1)} %collective-permute-done.12), channel_id=1, source_target_pairs={{0,2},{2,4},{4,6},{6,8},{8,10},{10,12},{12,14},{14,16},{16,18},{18... | collective-permute-start | bytes 49160 | tf_op jit(solution)/shard_map/ppermute | solution.py:26
  96.1 14.6 %collective-permute-start.14 = (bf16[128,64]{0,1:T(8,128)(2,1)}, bf16[128,64]{0,1:T(8,128)(2,1)}, u32[]{:S(2)}, u32[]{:S(2)}) collective-permute-start(bf16[128,64]{0,1:T(8,128)(2,1)} %collective-permute-done.13), channel_id=1, source_target_pairs={{0,2},{2,4},{4,6},{6,8},{8,10},{10,12},{12,14},{14,16},{16,18},{18... | collective-permute-start | bytes 49160 | tf_op jit(solution)/shard_map/ppermute | solution.py:26
  180.5 33.3 %copy-start.27 = (f32[2048]{0:T(1024)S(1)}, f32[2048]{0:T(1024)}, u32[]{:S(2)}) copy-start(f32[2048]{0:T(1024)} %param.30) | copy-start | bytes 24580
  342.6 98.6 %all-to-all-start.1 = ((bf16[16,64,2048]{2,1,0:T(8,128)(2,1)}), bf16[16,64,2048]{2,1,0:T(8,128)(2,1)}, u32[]{:S(2)}, u32[]{:S(2)}) async-start(bf16[16,64,2048]{2,1,0:T(8,128)(2,1)} %bitcast.83), calls=%async_computation.1 | async-start | bytes 8388608 | tf_op jit(solution)/shard_map/all_to_all | solution.py:236
  349.1 126.1 %reduce-scatter.2.cloned.1.call-start = ((), (), s32[]{:S(2)}) async-start(), calls=%async_computation.5 | async-start | bytes 786432 | tf_op jit(solution)/shard_map/reduce_scatter | solution.py:242
  (28 other events, 87.7 us)
Sparse Core Ops, SparseCore 0:
  73.7 77.1 all-gather.1
  182.2 29.1 all-reduce.1
  465.3 7.2 reduce-scatter.1
